TPU v7x, 32 devices: a whole 2x2x4 slice. The times are simulated.
32 devices in a mesh: prompt: 2 (over core), sample: 4 (over y, x), head: 4 (over z).
Axes of the slice: x: 2, y: 2, z: 4, core: 2. Of those that a mesh axis runs over, the one named last changes fastest.
Arguments:
- queries: bfloat16 [8, 64, 4096], P('sample', None, 'head'), may hold values from -8 to 8
- prompt_keys: bfloat16 [4096, 512], P(('prompt', 'sample'), 'head'), may hold values from -3 to 3
- prompt_values: bfloat16 [4096, 512], P(('prompt', 'sample'), 'head'), may hold values from -4 to 4
- resp_keys: bfloat16 [8, 2048, 512], P('sample', 'prompt', 'head'), may hold values from -3 to 3
- resp_values: bfloat16 [8, 2048, 512], P('sample', 'prompt', 'head'), may hold values from -4 to 4
- cotangent: bfloat16 [8, 64, 4096], P('sample', None, 'head'), may hold values from -4 to 4
- lengths: int32 [8], replicated, may hold values from 1 to 2048, as said below
- offsets: int32 [8], replicated, may hold values from 0 to 2047, as said below
Outputs:
- attended: bfloat16 [8, 64, 4096], P('sample', None, 'head')
- grad_queries: bfloat16 [8, 64, 4096], P('sample', 'prompt', 'head')
- grad_prompt_keys: bfloat16 [4096, 512], P(('prompt', 'sample'), 'head')
- grad_prompt_values: bfloat16 [4096, 512], P(('prompt', 'sample'), 'head')
- grad_resp_keys: bfloat16 [8, 2048, 512], P('sample', 'prompt', 'head')
- grad_resp_values: bfloat16 [8, 2048, 512], P('sample', 'prompt', 'head')
Inputs may be any that keep to these rules, and one draw needn't show every extreme that they name: `lengths`: some response has length 2048. `offsets`: each offset is below its response's length.
All inputs are finite; a program needn't handle non-finite values.
Results may differ from a plain program's by a relative error of at most 0.017.
Values may be sent and summed in bfloat16 or wider, within the bound.
A program may use at most 128 MiB of HBM per device.

v0:
```python
import math

import jax
import jax.numpy as jnp
from jax import lax
from jax.sharding import PartitionSpec as P

NEG = -1e30


def joined_2(shard, axis, combine):
    everything = jax.tree.map(lambda part: lax.all_gather(part, axis), shard)
    leading = jax.tree.map(lambda part: part[0], everything)

    def step(k, so_far):
        return combine(so_far, jax.tree.map(lambda part: part[k], everything))

    return lax.fori_loop(1, lax.axis_size(axis), step, leading)


def prompt_forward(rows, keys, values, scale):
    width = math.gcd(keys.shape[0], 512)
    depth = keys.shape[1]
    key_parts = keys.reshape(-1, width, depth)
    value_parts = values.reshape(-1, width, depth)

    def visit(carry, block):
        top, total, weighted = carry
        key_part, value_part = block
        scores = jnp.einsum("qd,kd->qk", rows, key_part, preferred_element_type=jnp.float32) * scale
        fresh = jnp.maximum(top, jnp.max(scores, axis=1))
        decay = jnp.exp(top - fresh)
        powers = jnp.exp(scores - fresh[:, None])
        total = total * decay + jnp.sum(powers, axis=1)
        weighted = weighted * decay[:, None] + jnp.dot(
            powers.astype(jnp.bfloat16), value_part, preferred_element_type=jnp.float32
        )
        return ((fresh, total, weighted), None)

    count = rows.shape[0]
    start = (
        jnp.full((count,), NEG, jnp.float32),
        jnp.zeros((count,), jnp.float32),
        jnp.zeros((count, depth), jnp.float32),
    )
    result, _ = lax.scan(visit, start, (key_parts, value_parts))
    return result


def prompt_backward(rows, grads, log_total, delta, keys, values, scale):
    width = math.gcd(keys.shape[0], 512)
    depth = keys.shape[1]
    key_parts = keys.reshape(-1, width, depth)
    value_parts = values.reshape(-1, width, depth)

    def visit(query_grad, block):
        key_part, value_part = block
        scores = jnp.einsum("qd,kd->qk", rows, key_part, preferred_element_type=jnp.float32) * scale
        weights = jnp.exp(scores - log_total[:, None])
        value_grad = jnp.einsum(
            "qk,qd->kd", weights.astype(jnp.bfloat16), grads, preferred_element_type=jnp.float32
        )
        weight_grad = jnp.einsum("qd,kd->qk", grads, value_part, preferred_element_type=jnp.float32)
        score_grad = (weights * (weight_grad - delta[:, None]) * scale).astype(jnp.bfloat16)
        query_grad = query_grad + jnp.dot(score_grad, key_part, preferred_element_type=jnp.float32)
        key_grad = jnp.einsum("qk,qd->kd", score_grad, rows, preferred_element_type=jnp.float32)
        return (query_grad, (key_grad, value_grad))

    query_grad, (key_grad, value_grad) = lax.scan(
        visit, jnp.zeros(rows.shape, jnp.float32), (key_parts, value_parts)
    )
    return (query_grad, key_grad.reshape(-1, depth), value_grad.reshape(-1, depth))


def own_scores(rows, keys, places, base, first, width, scale):
    key_part = lax.dynamic_slice_in_dim(keys, first, width, 1)
    scores = jnp.einsum("rqd,rkd->rqk", rows, key_part, preferred_element_type=jnp.float32) * scale
    key_places = base + first + jnp.arange(width, dtype=jnp.int32)
    seen = key_places[None, None, :] <= places[:, :, None]
    return (key_part, jnp.where(seen, scores, NEG), seen)


def own_forward(rows, keys, values, places, base, steps, width, scale):
    count, height, depth = rows.shape

    def visit(index, carry):
        top, total, weighted = carry
        first = index * width
        key_part, scores, seen = own_scores(rows, keys, places, base, first, width, scale)
        value_part = lax.dynamic_slice_in_dim(values, first, width, 1)
        fresh = jnp.maximum(top, jnp.max(scores, axis=2))
        decay = jnp.exp(top - fresh)
        powers = jnp.where(seen, jnp.exp(scores - fresh[..., None]), 0.0)
        total = total * decay + jnp.sum(powers, axis=2)
        weighted = weighted * decay[..., None] + jnp.einsum(
            "rqk,rkd->rqd",
            powers.astype(jnp.bfloat16),
            value_part,
            preferred_element_type=jnp.float32,
        )
        return (fresh, total, weighted)

    start = (
        jnp.full((count, height), NEG, jnp.float32),
        jnp.zeros((count, height), jnp.float32),
        jnp.zeros((count, height, depth), jnp.float32),
    )
    return lax.fori_loop(0, steps, visit, start)


def own_backward(rows, grads, log_total, delta, keys, values, places, base, steps, width, scale):

    def visit(index, carry):
        query_grad, key_grads, value_grads = carry
        first = index * width
        key_part, scores, seen = own_scores(rows, keys, places, base, first, width, scale)
        value_part = lax.dynamic_slice_in_dim(values, first, width, 1)
        weights = jnp.where(seen, jnp.exp(scores - log_total[..., None]), 0.0)
        value_grad = jnp.einsum(
            "rqk,rqd->rkd", weights.astype(jnp.bfloat16), grads, preferred_element_type=jnp.float32
        )
        weight_grad = jnp.einsum(
            "rqd,rkd->rqk", grads, value_part, preferred_element_type=jnp.float32
        )
        score_grad = (weights * (weight_grad - delta[..., None]) * scale).astype(jnp.bfloat16)
        query_grad = query_grad + jnp.einsum(
            "rqk,rkd->rqd", score_grad, key_part, preferred_element_type=jnp.float32
        )
        key_grad = jnp.einsum("rqk,rqd->rkd", score_grad, rows, preferred_element_type=jnp.float32)
        key_grads = lax.dynamic_update_slice_in_dim(key_grads, key_grad, first, 1)
        value_grads = lax.dynamic_update_slice_in_dim(value_grads, value_grad, first, 1)
        return (query_grad, key_grads, value_grads)

    start = (
        jnp.zeros(rows.shape, jnp.float32),
        jnp.zeros(keys.shape, jnp.float32),
        jnp.zeros(values.shape, jnp.float32),
    )
    return lax.fori_loop(0, steps, visit, start)


def local(queries, prompt_keys, prompt_values, resp_keys, resp_values, cotangent, lengths, offsets):
    own_count, window, wide = queries.shape
    depth = prompt_keys.shape[1]
    group = wide // depth
    height = window * group
    span = resp_keys.shape[1]
    scale = 1.0 / math.sqrt(depth)
    first_own = lax.axis_index("sample") * own_count
    line = jnp.arange(window, dtype=jnp.int32)
    live_all = offsets[:, None] + line[None, :] < lengths[:, None]
    live_own = lax.dynamic_slice_in_dim(live_all, first_own, own_count, 0)
    own_offsets = lax.dynamic_slice_in_dim(offsets, first_own, own_count, 0)
    places = own_offsets[:, None] + (jnp.arange(height, dtype=jnp.int32) // group)[None, :]
    width = math.gcd(span, 256)
    base = lax.axis_index("prompt") * span
    steps = span // width
    own_rows = queries.reshape(own_count, height, depth)
    own_top, own_total, own_weighted = own_forward(
        own_rows, resp_keys, resp_values, places, base, steps, width, scale
    )
    own_part = (
        own_top.reshape(own_count, window, group),
        own_total.reshape(own_count, window, group),
        own_weighted.reshape(own_count, window, wide),
    )

    def combine(left, right):
        fresh = jnp.maximum(left[0], right[0])
        left_decay = jnp.exp(left[0] - fresh)
        right_decay = jnp.exp(right[0] - fresh)
        total = left[1] * left_decay + right[1] * right_decay
        shape = left[2].shape
        split_shape = shape[:-1] + (group, depth)
        weighted = (
            left[2].reshape(split_shape) * left_decay[..., None]
            + right[2].reshape(split_shape) * right_decay[..., None]
        )
        return (fresh, total, weighted.reshape(shape))

    gathered = (
        lax.all_gather(prompt_keys, "sample", axis=0, tiled=True),
        lax.all_gather(prompt_values, "sample", axis=0, tiled=True),
    )
    top, total, weighted = prompt_forward(
        queries.reshape(own_count * height, depth), gathered[0], gathered[1], scale
    )
    prompt_part = (
        top.reshape(own_count, window, group),
        total.reshape(own_count, window, group),
        weighted.reshape(own_count, window, wide),
    )
    joined = combine(prompt_part, own_part)
    merged = joined_2((joined[0], joined[1], joined[2]), "prompt", combine)
    output_own = (
        merged[2].reshape(own_count, window, group, depth) / merged[1][..., None]
    ).reshape(own_count, window, wide)
    log_own = merged[0] + jnp.log(merged[1])
    attended = (output_own * live_own.astype(jnp.float32)[..., None]).astype(jnp.bfloat16)
    grads_own = cotangent * live_own.astype(jnp.bfloat16)[..., None]
    delta_own = jnp.sum(
        (grads_own.astype(jnp.float32) * output_own).reshape(own_count, window, group, depth),
        axis=3,
    )
    own_query_grad, own_key_grad, own_value_grad = own_backward(
        own_rows,
        grads_own.reshape(own_count, height, depth),
        log_own.reshape(own_count, height),
        delta_own.reshape(own_count, height),
        resp_keys,
        resp_values,
        places,
        base,
        steps,
        width,
        scale,
    )
    own_query_grad = own_query_grad.reshape(own_count, window, wide)
    query_grad, key_grad, value_grad = prompt_backward(
        queries.reshape(own_count * height, depth),
        grads_own.reshape(own_count * height, depth),
        log_own.reshape(own_count * height),
        delta_own.reshape(own_count * height),
        gathered[0],
        gathered[1],
        scale,
    )
    key_sum, value_sum = (
        lax.psum_scatter(key_grad, "sample", scatter_dimension=0, tiled=True),
        lax.psum_scatter(value_grad, "sample", scatter_dimension=0, tiled=True),
    )
    sample_terms = query_grad.reshape(own_count, window, wide) + own_query_grad
    grad_queries = lax.psum_scatter(sample_terms, "prompt", scatter_dimension=1, tiled=True).astype(
        jnp.bfloat16
    )
    return (
        attended,
        grad_queries,
        key_sum.astype(jnp.bfloat16),
        value_sum.astype(jnp.bfloat16),
        own_key_grad.astype(jnp.bfloat16),
        own_value_grad.astype(jnp.bfloat16),
    )


def solution(mesh):
    return jax.shard_map(
        local,
        mesh=mesh,
        in_specs=(
            P("sample", None, "head"),
            P(("prompt", "sample"), "head"),
            P(("prompt", "sample"), "head"),
            P("sample", "prompt", "head"),
            P("sample", "prompt", "head"),
            P("sample", None, "head"),
            P(),
            P(),
        ),
        out_specs=(
            P("sample", None, "head"),
            P("sample", "prompt", "head"),
            P(("prompt", "sample"), "head"),
            P(("prompt", "sample"), "head"),
            P("sample", "prompt", "head"),
            P("sample", "prompt", "head"),
        ),
        check_vma=False,
    )
```

profile of v0, /device:TPU:0, one launch (start us, length us, event | category | flops | bytes accessed | tf_op | source)
XLA Modules:
  0.0 214.7 jit_solution(10302813589777007516)
XLA Ops:
  10.2 12.5 %while.76 = (s32[]{:T(128)}, f32[2,512]{1,0:T(2,128)S(1)}, f32[2,512]{1,0:T(2,128)S(1)}, f32[2,512,128]{2,1,0:T(8,128)S(1)}, s32[]{:T(128)}, /*index=5*/bf16[2,1...) while((s32[]{:T(128)}, f32[2,512]{1,0:T(2,128)S(1)}, ...), condition=%wide.region_7.8_spmd.clone, body=%wide.region_4.7_spmd.clone.sunk | while | flops 137763072 | bytes 4806887 | solution.py:108
  22.7 12.2 %all_gather.17 = bf16[2048,128]{1,0:T(8,128)(2,1)} all-gather(bf16[512,128]{1,0:T(8,128)(2,1)S(1)} %copy-done.12), channel_id=1, replica_groups=mesh['prompt'=2,'sample'=4,'head'=4] {'sample'}, dimensions={0}, use_global_device_ids=true | all-gather | bytes 655360 | tf_op jit(solution)/shard_map/all_gather | solution.py:182
  34.9 11.2 %all_gather.18 = bf16[2048,128]{1,0:T(8,128)(2,1)} all-gather(bf16[512,128]{1,0:T(8,128)(2,1)S(1)} %copy-done.13), channel_id=1, replica_groups=mesh['prompt'=2,'sample'=4,'head'=4] {'sample'}, dimensions={0}, use_global_device_ids=true | all-gather | bytes 655360 | tf_op jit(solution)/shard_map/all_gather | solution.py:183
  46.1 13.3 %while.75 = (s32[]{:T(128)}, f32[1024]{0:T(1024)S(1)}, f32[1024]{0:T(1024)S(1)}, f32[1024,128]{1,0:T(8,128)S(1)}, bf16[4,512,128]{2,1,0:T(8,128)(2,1)}, /*index=...) while((s32[]{:T(128)}, f32[1024]{0:T(1024)S(1)}, ...), condition=%wide.region_3.4_spmd.clone, body=%wide.region_0.3_spmd.clone.sunk | while | flops 273028096 | bytes 7929977 | solution.py:46
  47.9 1.5 convolution_add_fusion.10
  51.2 1.5 convolution_add_fusion.10
  54.6 1.5 convolution_add_fusion.10
  57.9 1.5 convolution_add_fusion.10
  62.1 1.8 all_gather.20
  64.0 1.8 all_gather.21
  67.4 3.4 %all-gather.2.cloned.1.call-done = f32[2,2,64,1024]{3,2,1,0:T(8,128)} async-done(((f32[1,2,64,1024]{3,2,1,0:T(8,128)}), f32[2,2,64,1024]{3,2,1,0:T(8,128)}) %all-gather.2.cloned.1.call-update) | async-done | bytes 1048592 | tf_op jit(solution)/shard_map/all_gather | solution.py:12
  70.8 2.3 %convert_multiply_fusion = (f32[2,64,1024]{2,1,0:T(8,128)S(1)}, bf16[2,64,1024]{2,1,0:T(8,128)(2,1)S(1)}, f32[2,64,1024]{2,1,0:T(8,128)}) fusion(bf16[2,64,1024]{2,1,0:T(8,128)(2,1)S(1)} %copy-done.11, bf16[2,64]{1,0:T(2,128)(2,1)S(1)} %get-tuple-element.788, f32[2,64,1024]{2,1,0:T(8,128)S(1)} %div.22, f32[2,64,1024]{2,1,0:T(8,128)S(1)} %mul.242, ...), kind=kLoop, calls=%fused_computation.97 | loop fusion | flops 917504 | bytes 4194560 | tf_op jit(solution)/shard_map/mul | solution.py:202
  75.7 30.6 %while.77 = (s32[]{:T(128)}, f32[1024,128]{1,0:T(8,128)}, f32[4,512,128]{2,1,0:T(8,128)}, f32[4,512,128]{2,1,0:T(8,128)}, bf16[4,512,128]{2,1,0:T(8,128)(2,1)}, ...) while((s32[]{:T(128)}, f32[1024,128]{1,0:T(8,128)}, ...), condition=%wide.wide.region_10.11_spmd.clone, body=%wide.wide.region_9.10_spmd.clone.sunk | while | flops 676069376 | bytes 14561507 | solution.py:69
  78.7 2.2 %convolution_add_fusion.12 = f32[1024,128]{1,0:T(8,128)} fusion(bf16[512,1024]{1,0:T(8,128)(2,1)S(1)} %multiply_convert_fusion.4, f32[1024,128]{1,0:T(8,128)} %get-tuple-element.1247, pred[]{:T(512)S(6)} %compare.20, bf16[4,512,128]{2,1,0:T(8,128)(2,1)} %get-tuple-element.1264, s32[]{:T(128)S(6)} %copy.77), kind=kOutput, calls=%fused_computation.49.clone.clone.1 | convolution fusion | flops 134479872 | bytes 2228229 | tf_op jit(solution)/shard_map/while/body/eval_jaxpr/dot_general | solution.py:65
  86.2 2.4 %convolution_add_fusion.12 = f32[1024,128]{1,0:T(8,128)} fusion(bf16[512,1024]{1,0:T(8,128)(2,1)S(1)} %multiply_convert_fusion.4, f32[1024,128]{1,0:T(8,128)} %get-tuple-element.1247, pred[]{:T(512)S(6)} %compare.20, bf16[4,512,128]{2,1,0:T(8,128)(2,1)} %get-tuple-element.1264, s32[]{:T(128)S(6)} %copy.77), kind=kOutput, calls=%fused_computation.49.clone.clone.1 | convolution fusion | flops 134479872 | bytes 2228229 | tf_op jit(solution)/shard_map/while/body/eval_jaxpr/dot_general | solution.py:65
  93.8 2.4 %convolution_add_fusion.12 = f32[1024,128]{1,0:T(8,128)} fusion(bf16[512,1024]{1,0:T(8,128)(2,1)S(1)} %multiply_convert_fusion.4, f32[1024,128]{1,0:T(8,128)} %get-tuple-element.1247, pred[]{:T(512)S(6)} %compare.20, bf16[4,512,128]{2,1,0:T(8,128)(2,1)} %get-tuple-element.1264, s32[]{:T(128)S(6)} %copy.77), kind=kOutput, calls=%fused_computation.49.clone.clone.1 | convolution fusion | flops 134479872 | bytes 2228229 | tf_op jit(solution)/shard_map/while/body/eval_jaxpr/dot_general | solution.py:65
  101.5 2.4 %convolution_add_fusion.12 = f32[1024,128]{1,0:T(8,128)} fusion(bf16[512,1024]{1,0:T(8,128)(2,1)S(1)} %multiply_convert_fusion.4, f32[1024,128]{1,0:T(8,128)} %get-tuple-element.1247, pred[]{:T(512)S(6)} %compare.20, bf16[4,512,128]{2,1,0:T(8,128)(2,1)} %get-tuple-element.1264, s32[]{:T(128)S(6)} %copy.77), kind=kOutput, calls=%fused_computation.49.clone.clone.1 | convolution fusion | flops 134479872 | bytes 2228229 | tf_op jit(solution)/shard_map/while/body/eval_jaxpr/dot_general | solution.py:65
  109.3 24.5 %while.78 = (s32[]{:T(128)}, f32[2,512,128]{2,1,0:T(8,128)S(1)}, bf16[2,1024,128]{2,1,0:T(8,128)(2,1)}, bf16[2,1024,128]{2,1,0:T(8,128)(2,1)}, s32[]{:T(128)}, /...) while((s32[]{:T(128)}, f32[2,512,128]{2,1,0:T(8,128)S(1)}, ...), condition=%wide.wide.region_12.13_spmd.clone, body=%wide.wide.region_11.12_spmd.clone.sunk | while | flops 338429184 | bytes 11948369 | solution.py:139
  136.9 7.2 %reduce-scatter.4.cloned.1.call-done = f32[2,32,1024]{2,1,0:T(8,128)} async-done(((f32[2,64,1024]{2,1,0:T(8,128)}), f32[2,32,1024]{2,1,0:T(8,128)}) %reduce-scatter.4.cloned.1.call-update) | async-done | bytes 262160 | tf_op jit(solution)/shard_map/reduce_scatter | solution.py:233
  144.0 1.6 convert_element_type.63
  145.6 30.4 %reduce-scatter.6.cloned.1.call-done = f32[512,128]{1,0:T(8,128)} async-done(((f32[2048,128]{1,0:T(8,128)}), f32[512,128]{1,0:T(8,128)}) %reduce-scatter.6.cloned.1.call-update) | async-done | bytes 262160 | tf_op jit(solution)/shard_map/reduce_scatter | solution.py:229
  176.1 1.6 convert_element_type.64
  177.7 28.9 %reduce-scatter.8.cloned.1.call-done = f32[512,128]{1,0:T(8,128)} async-done(((f32[2048,128]{1,0:T(8,128)}), f32[512,128]{1,0:T(8,128)}) %reduce-scatter.8.cloned.1.call-update) | async-done | bytes 262160 | tf_op jit(solution)/shard_map/reduce_scatter | solution.py:230
  206.6 1.6 convert_element_type.65
  (220 shorter events, 80.1 us)
Async XLA Ops:
  7.2 63.7 %all-gather.2.cloned.1.call-start = ((), (), s32[]{:S(2)}) async-start(), calls=%async_computation.3 | async-start | bytes 1572864 | tf_op jit(solution)/shard_map/all_gather | solution.py:12
  10.2 12.5 %copy-start.12 = (bf16[512,128]{1,0:T(8,128)(2,1)S(1)}, bf16[512,128]{1,0:T(8,128)(2,1)}, u32[]{:S(2)}) copy-start(bf16[512,128]{1,0:T(8,128)(2,1)} %param.17) | copy-start | bytes 393220
  10.2 24.7 %copy-start.13 = (bf16[512,128]{1,0:T(8,128)(2,1)S(1)}, bf16[512,128]{1,0:T(8,128)(2,1)}, u32[]{:S(2)}) copy-start(bf16[512,128]{1,0:T(8,128)(2,1)} %param.18) | copy-start | bytes 393220
  22.7 23.4 %copy-start.4 = (bf16[2,512,128]{2,1,0:T(8,128)(2,1)}, bf16[2,512,128]{2,1,0:T(8,128)(2,1)S(1)}, u32[]{:S(2)}) copy-start(bf16[2,512,128]{2,1,0:T(8,128)(2,1)S(1)} %get-tuple-element.1337) | copy-start | bytes 786436
  61.4 82.6 %reduce-scatter.4.cloned.1.call-start = ((), (), s32[]{:S(2)}) async-start(), calls=%async_computation.4 | async-start | bytes 786432 | tf_op jit(solution)/shard_map/reduce_scatter | solution.py:233
  66.4 4.4 %copy-start.11 = (bf16[2,64,1024]{2,1,0:T(8,128)(2,1)S(1)}, bf16[2,64,1024]{2,1,0:T(8,128)(2,1)}, u32[]{:S(2)}) copy-start(bf16[2,64,1024]{2,1,0:T(8,128)(2,1)} %param.21) | copy-start | bytes 786436
  75.7 1.4 copy-start.1
  78.6 3.4 %copy-start.2 = (bf16[1024,128]{1,0:T(8,128)(2,1)S(1)}, bf16[1024,128]{1,0:T(8,128)(2,1)}, u32[]{:S(2)}) copy-start(bf16[1024,128]{1,0:T(8,128)(2,1)} %get-tuple-element.1268) | copy-start | bytes 786436 | tf_op jit(solution)/shard_map/while
  83.2 1.4 copy-start.1
  86.1 3.6 %copy-start.2 = (bf16[1024,128]{1,0:T(8,128)(2,1)S(1)}, bf16[1024,128]{1,0:T(8,128)(2,1)}, u32[]{:S(2)}) copy-start(bf16[1024,128]{1,0:T(8,128)(2,1)} %get-tuple-element.1268) | copy-start | bytes 786436 | tf_op jit(solution)/shard_map/while
  90.9 1.4 copy-start.1
  93.8 3.6 %copy-start.2 = (bf16[1024,128]{1,0:T(8,128)(2,1)S(1)}, bf16[1024,128]{1,0:T(8,128)(2,1)}, u32[]{:S(2)}) copy-start(bf16[1024,128]{1,0:T(8,128)(2,1)} %get-tuple-element.1268) | copy-start | bytes 786436 | tf_op jit(solution)/shard_map/while
  98.6 1.4 copy-start.1
  101.5 3.6 %copy-start.2 = (bf16[1024,128]{1,0:T(8,128)(2,1)S(1)}, bf16[1024,128]{1,0:T(8,128)(2,1)}, u32[]{:S(2)}) copy-start(bf16[1024,128]{1,0:T(8,128)(2,1)} %get-tuple-element.1268) | copy-start | bytes 786436 | tf_op jit(solution)/shard_map/while
  106.3 2.9 %copy-start = (bf16[2,512,128]{2,1,0:T(8,128)(2,1)S(1)}, bf16[2,512,128]{2,1,0:T(8,128)(2,1)}, u32[]{:S(2)}) copy-start(bf16[2,512,128]{2,1,0:T(8,128)(2,1)} %reshape.315) | copy-start | bytes 786436
  106.3 3.0 %copy-start.3 = (f32[2,512,128]{2,1,0:T(8,128)S(1)}, f32[2,512,128]{2,1,0:T(8,128)}, u32[]{:S(2)}) copy-start(f32[2,512,128]{2,1,0:T(8,128)} %custom-call.7) | copy-start | bytes 1572868
  106.3 3.0 %copy-start.5 = (bf16[2,512,128]{2,1,0:T(8,128)(2,1)S(1)}, bf16[2,512,128]{2,1,0:T(8,128)(2,1)}, u32[]{:S(2)}) copy-start(bf16[2,512,128]{2,1,0:T(8,128)(2,1)} %copy-done.4) | copy-start | bytes 786436
  111.9 2.4 %copy-start.9 = (bf16[2,1024,128]{2,1,0:T(8,128)(2,1)S(1)}, bf16[2,1024,128]{2,1,0:T(8,128)(2,1)}, u32[]{:S(2)}) copy-start(bf16[2,1024,128]{2,1,0:T(8,128)(2,1)} %get-tuple-element.1296) | copy-start | bytes 1572868 | tf_op jit(solution)/shard_map/while
  118.0 2.4 %copy-start.9 = (bf16[2,1024,128]{2,1,0:T(8,128)(2,1)S(1)}, bf16[2,1024,128]{2,1,0:T(8,128)(2,1)}, u32[]{:S(2)}) copy-start(bf16[2,1024,128]{2,1,0:T(8,128)(2,1)} %get-tuple-element.1296) | copy-start | bytes 1572868 | tf_op jit(solution)/shard_map/while
  124.1 2.4 %copy-start.9 = (bf16[2,1024,128]{2,1,0:T(8,128)(2,1)S(1)}, bf16[2,1024,128]{2,1,0:T(8,128)(2,1)}, u32[]{:S(2)}) copy-start(bf16[2,1024,128]{2,1,0:T(8,128)(2,1)} %get-tuple-element.1296) | copy-start | bytes 1572868 | tf_op jit(solution)/shard_map/while
  130.2 2.4 %copy-start.9 = (bf16[2,1024,128]{2,1,0:T(8,128)(2,1)S(1)}, bf16[2,1024,128]{2,1,0:T(8,128)(2,1)}, u32[]{:S(2)}) copy-start(bf16[2,1024,128]{2,1,0:T(8,128)(2,1)} %get-tuple-element.1296) | copy-start | bytes 1572868 | tf_op jit(solution)/shard_map/while
  133.8 2.2 %copy-start.6 = (f32[2,64,1024]{2,1,0:T(8,128)S(1)}, f32[2,64,1024]{2,1,0:T(8,128)}, u32[]{:S(2)}) copy-start(f32[2,64,1024]{2,1,0:T(8,128)} %get-tuple-element.774) | copy-start | bytes 1572868
  134.7 41.3 %reduce-scatter.6.cloned.1.call-start = ((), (), s32[]{:S(2)}) async-start(), calls=%async_computation.5 | async-start | bytes 1310720 | tf_op jit(solution)/shard_map/reduce_scatter | solution.py:229
  135.5 71.1 %reduce-scatter.8.cloned.1.call-start = ((), (), s32[]{:S(2)}) async-start(), calls=%async_computation.6 | async-start | bytes 1310720 | tf_op jit(solution)/shard_map/reduce_scatter | solution.py:230
  (8 other events, 7.0 us)
Sparse Core Ops, SparseCore 0:
  61.5 9.2 all-gather.1
  134.9 9.1 reduce-scatter.3
  147.2 28.8 reduce-scatter.5
  178.8 27.7 reduce-scatter.7
where the time goes:
time: 216 us; the launch traced here: 215 us
  matrix products  73.6 us (34%)
  waiting for transfers between devices  71.2 us (33%)
  blocking collectives  27 us (12%)
  local copies, waits for them, and re-layouts  14.5 us (7%)
  between operations  14.2 us (7%)
  other arithmetic  13.4 us (6%)
    reduce_scatter x1, waiting for transfers between devices, local(): lax.psum_scatter(key_grad, 'sample', scatter_dimension=0, tiled=True)  30.4 us
    reduce_scatter x1, waiting for transfers between devices, local(): lax.psum_scatter(value_grad, 'sample', scatter_dimension=0, tiled=True)  28.9 us
    all_gather x1, blocking collectives, local(): lax.all_gather(prompt_keys, 'sample', axis=0, tiled=True)  12.2 us
    all_gather x1, blocking collectives, local(): lax.all_gather(prompt_values, 'sample', axis=0, tiled=True)  11.2 us
    dot_general x8, matrix products, visit(): jnp.einsum('qd,kd->qk', rows, key_part, preferred_element_type=jnp.float32)  10.9 us
    dot_general x8, matrix products, own_scores(): jnp.einsum('rqd,rkd->rqk', rows, key_part, preferred_element_type=jnp.flo...  10.2 us
    dot_general x4, matrix products, visit(): jnp.dot(score_grad, key_part, preferred_element_type=jnp.float32)  9.47 us
    reduce_scatter x1, waiting for transfers between devices, local(): lax.psum_scatter(sample_terms, 'prompt', scatter_dimension=1, tiled=True)  7.15 us
  transfers between devices with their start and end apart: 4, of which 4 were waited for; matrix products, arithmetic and copies ran while one was open for 3% of the time, Pallas kernels for 0%

commit v1 on v0

v1 whole, which is shorter than its diff:
```python
import functools
import math

import jax
import jax.numpy as jnp
from jax import lax
from jax.experimental import pallas as pl
from jax.experimental.pallas import tpu as pltpu
from jax.sharding import PartitionSpec as P

NEG = -1e30
MESH = pl.DeviceIdType.MESH
F32 = jnp.float32
BF16 = jnp.bfloat16


def dot(a, b):
    return jnp.dot(a, b, preferred_element_type=F32)


def dot_nt(a, b):
    return lax.dot_general(a, b, (((1,), (1,)), ((), ())), preferred_element_type=F32)


def kernel(
    n_p,
    n_s,
    offsets,
    lengths,
    q_ref,
    pk_ref,
    pv_ref,
    rk_ref,
    rv_ref,
    g_ref,
    att_ref,
    gq_ref,
    gpk_ref,
    gpv_ref,
    grk_ref,
    grv_ref,
    kv,
    qrows,
    grows,
    g_t,
    p_all,
    p_own,
    ds,
    g_scaled,
    small_t,
    acc,
    acc_in,
    out_t,
    tops,
    stats,
    gq_t,
    kvg_own,
    kvg_out,
    kvg_in,
    gq_out,
    gq_in,
    kv_send,
    kv_recv,
    acc_send,
    acc_recv,
    kvg_send,
    kvg_recv,
    gq_send,
    gq_recv,
):
    count, window, wide = q_ref.shape
    width, depth = pk_ref.shape
    span = rk_ref.shape[1]
    group = wide // depth
    height = window * group
    rows = count * height
    tile = math.gcd(height, 256)
    per = height // tile
    scale = 1.0 / math.sqrt(depth)
    c = scale * math.log2(math.e)
    me_s = lax.axis_index("sample")
    me_p = lax.axis_index("prompt")
    part = window // n_p

    def to_sample(k):
        if n_s == 4:
            return ((me_s // 2 + k // 2) % 2) * 2 + (me_s % 2 + k % 2) % 2
        return (me_s + k) % n_s

    def from_sample(k):
        if n_s == 4:
            return to_sample(k)
        return (me_s + n_s - k) % n_s

    barrier = pltpu.get_barrier_semaphore()
    for k in range(1, n_s):
        pl.semaphore_signal(barrier, inc=1, device_id={"sample": to_sample(k)}, device_id_type=MESH)
    for k in range(1, n_p):
        pl.semaphore_signal(
            barrier, inc=1, device_id={"prompt": (me_p + k) % n_p}, device_id_type=MESH
        )
    pl.semaphore_wait(barrier, n_s - 1 + n_p - 1)

    kv_copies = {}
    for k in range(1, n_s):
        for j, ref in enumerate((pk_ref, pv_ref)):
            copy = pltpu.make_async_remote_copy(
                src_ref=ref,
                dst_ref=kv.at[k - 1, j],
                send_sem=kv_send.at[k - 1, j],
                recv_sem=kv_recv.at[k - 1, j],
                device_id={"sample": to_sample(k)},
                device_id_type=MESH,
            )
            copy.start()
            kv_copies[k, j] = copy

    own = [(offsets[me_s * count + r], lengths[me_s * count + r]) for r in range(count)]
    line = lax.broadcasted_iota(jnp.int32, (window, 1), 0)
    for r in range(count):
        live = own[r][0] + line < own[r][1]
        for h in range(group):
            at = pl.ds(r * height + h * window, window)
            head = pl.ds(h * depth, depth)
            qrows[at, :] = q_ref[r, :, head]
            grows[at, :] = jnp.where(live, g_ref[r, :, head].astype(F32), 0.0).astype(BF16)
    for i in range(rows // tile):
        at = pl.ds(i * tile, tile)
        g_t[:, at] = grows[at, :].T

    def forward(seg, keys, values, p_ref, low, high, mask, first):
        size = keys.shape[0]
        small_t[:, :size] = values[...].T

        def visit(i, _):
            at = pl.ds(pl.multiple_of(i * tile, tile), tile)
            scores = dot_nt(keys[...], qrows[at, :])
            if mask is not None:
                scores = mask(scores)
            top = jnp.max(scores, axis=0, keepdims=True)
            powers = jnp.exp2((scores - top) * c)
            total = jnp.sum(powers, axis=0, keepdims=True)
            low_powers = powers.astype(BF16)
            p_ref[:, at] = low_powers
            weighted = dot(small_t[:, :size], low_powers)
            tops[seg : seg + 1, at] = top
            if first:
                acc[0:depth, at] = weighted
                acc[depth : depth + 1, at] = top
                acc[depth + 1 : depth + 2, at] = total
            else:
                before = acc[depth : depth + 1, at]
                fresh = jnp.maximum(before, top)
                old = jnp.exp2((before - fresh) * c)
                new = jnp.exp2((top - fresh) * c)
                acc[0:depth, at] = acc[0:depth, at] * old + weighted * new
                acc[depth : depth + 1, at] = fresh
                acc[depth + 1 : depth + 2, at] = acc[depth + 1 : depth + 2, at] * old + total * new
            return 0

        lax.fori_loop(low, high, visit, 0)

    for r in range(count):
        key_place = me_p * span + lax.broadcasted_iota(jnp.int32, (span, 1), 0)
        row_place = own[r][0] + lax.broadcasted_iota(jnp.int32, (1, tile), 1) % window

        def mask(scores):
            return jnp.where(key_place <= row_place, scores, NEG)

        forward(n_s, rk_ref.at[r], rv_ref.at[r], p_own, r * per, (r + 1) * per, mask, True)
    forward(0, pk_ref, pv_ref, p_all.at[0], 0, count * per, None, False)
    for k in range(1, n_s):
        kv_copies[k, 0].wait_recv()
        kv_copies[k, 1].wait_recv()
        forward(
            k, kv.at[k - 1, 0], kv.at[k - 1, 1], p_all.at[k], 0, count * per, None, False
        )

    acc_copies = []
    for k in range(1, n_p):
        copy = pltpu.make_async_remote_copy(
            src_ref=acc,
            dst_ref=acc_in.at[k - 1],
            send_sem=acc_send.at[k - 1],
            recv_sem=acc_recv.at[k - 1],
            device_id={"prompt": (me_p + k) % n_p},
            device_id_type=MESH,
        )
        copy.start()
        acc_copies.append(copy)
    for copy in acc_copies:
        copy.wait_recv()

    for i in range(rows // tile):
        at = pl.ds(i * tile, tile)
        top = acc[depth : depth + 1, at]
        for k in range(n_p - 1):
            top = jnp.maximum(top, acc_in[k, depth : depth + 1, at])
        decay = jnp.exp2((acc[depth : depth + 1, at] - top) * c)
        total = acc[depth + 1 : depth + 2, at] * decay
        weighted = acc[0:depth, at] * decay
        for k in range(n_p - 1):
            decay = jnp.exp2((acc_in[k, depth : depth + 1, at] - top) * c)
            total = total + acc_in[k, depth + 1 : depth + 2, at] * decay
            weighted = weighted + acc_in[k, 0:depth, at] * decay
        inverse = 1.0 / total
        output = weighted * inverse
        out_t[:, at] = output
        stats[0:1, at] = top
        stats[1:2, at] = inverse
        gq_t[:, at] = jnp.zeros((depth, tile), F32)
        r = i // per
        live = own[r][0] + line < own[r][1]
        by_row = output.T
        for part_h in range(tile // window):
            h = (i % per) * (tile // window) + part_h
            block = by_row[part_h * window : (part_h + 1) * window]
            att_ref[r, :, pl.ds(h * depth, depth)] = jnp.where(live, block, 0.0).astype(BF16)

    def backward(seg, keys, values, p_ref, low, high):
        size = keys.shape[0]
        small_t[:, :size] = keys[...].T

        def visit(i, _):
            at = pl.ds(pl.multiple_of(i * tile, tile), tile)
            factor = jnp.exp2((tops[seg : seg + 1, at] - stats[0:1, at]) * c) * stats[1:2, at]
            grads = (g_t[:, at].astype(F32) * factor).astype(BF16)
            delta = jnp.sum(grads.astype(F32) * out_t[:, at], axis=0, keepdims=True)
            g_scaled[at, :] = grads.T
            weight_grad = dot(values[...], grads)
            score_grad = (p_ref[:, at].astype(F32) * (weight_grad - delta)).astype(BF16)
            ds[:size, at] = score_grad
            gq_t[:, at] += dot(small_t[:, :size], score_grad)
            return 0

        lax.fori_loop(low, high, visit, 0)
        span_rows = slice(low * tile, high * tile)
        value_grad = dot(p_ref[:, span_rows], g_scaled[span_rows, :])
        key_grad = dot(ds[:size, span_rows], qrows[span_rows, :]) * scale
        return key_grad, value_grad

    kvg_copies = []
    for k in range(n_s - 1, 0, -1):
        key_grad, value_grad = backward(
            k, kv.at[k - 1, 0], kv.at[k - 1, 1], p_all.at[k], 0, count * per
        )
        kvg_out[k - 1, 0] = key_grad.astype(BF16)
        kvg_out[k - 1, 1] = value_grad.astype(BF16)
        copy = pltpu.make_async_remote_copy(
            src_ref=kvg_out.at[k - 1],
            dst_ref=kvg_in.at[k - 1],
            send_sem=kvg_send.at[k - 1],
            recv_sem=kvg_recv.at[k - 1],
            device_id={"sample": from_sample(k)},
            device_id_type=MESH,
        )
        copy.start()
        kvg_copies.append(copy)
    key_grad, value_grad = backward(0, pk_ref, pv_ref, p_all.at[0], 0, count * per)
    kvg_own[0] = key_grad
    kvg_own[1] = value_grad
    for r in range(count):
        key_grad, value_grad = backward(
            n_s, rk_ref.at[r], rv_ref.at[r], p_own, r * per, (r + 1) * per
        )
        grk_ref[r] = key_grad.astype(BF16)
        grv_ref[r] = value_grad.astype(BF16)

    for i in range(rows // tile):
        at = pl.ds(i * tile, tile)
        r = i // per
        by_row = gq_t[:, at].T * scale
        for part_h in range(tile // window):
            h = (i % per) * (tile // window) + part_h
            for to in range(n_p):
                first = part_h * window + to * part
                gq_out[to, r, :, pl.ds(h * depth, depth)] = by_row[first : first + part]
    gq_copies = []
    for k in range(1, n_p):
        to = (me_p + k) % n_p
        copy = pltpu.make_async_remote_copy(
            src_ref=gq_out.at[to],
            dst_ref=gq_in.at[k - 1],
            send_sem=gq_send.at[k - 1],
            recv_sem=gq_recv.at[k - 1],
            device_id={"prompt": to},
            device_id_type=MESH,
        )
        copy.start()
        gq_copies.append(copy)
    for copy in kvg_copies:
        copy.wait_recv()
    for j, ref in enumerate((gpk_ref, gpv_ref)):
        total = kvg_own[j]
        for k in range(n_s - 1):
            total = total + kvg_in[k, j].astype(F32)
        ref[...] = total.astype(BF16)
    for copy in gq_copies:
        copy.wait_recv()
    total = gq_out[me_p]
    for k in range(n_p - 1):
        total = total + gq_in[k]
    gq_ref[...] = total.astype(BF16)

    for copy in kv_copies.values():
        copy.wait_send()
    for copy in acc_copies + kvg_copies + gq_copies:
        copy.wait_send()


def local(n_p, n_s, queries, prompt_keys, prompt_values, resp_keys, resp_values, cotangent, lengths, offsets):
    count, window, wide = queries.shape
    width, depth = prompt_keys.shape
    span = resp_keys.shape[1]
    rows = count * window * (wide // depth)
    tall = depth + 8
    vmem = pl.BlockSpec(memory_space=pltpu.VMEM)
    smem = pl.BlockSpec(memory_space=pltpu.SMEM)
    shape = jax.ShapeDtypeStruct
    dma = pltpu.SemaphoreType.DMA
    peers = max(n_p - 1, 1)
    others = max(n_s - 1, 1)
    scratch = [
        pltpu.VMEM((others, 2, width, depth), BF16),
        pltpu.VMEM((rows, depth), BF16),
        pltpu.VMEM((rows, depth), BF16),
        pltpu.VMEM((depth, rows), BF16),
        pltpu.VMEM((n_s, width, rows), BF16),
        pltpu.VMEM((span, rows), BF16),
        pltpu.VMEM((max(span, width), rows), BF16),
        pltpu.VMEM((rows, depth), BF16),
        pltpu.VMEM((depth, max(span, width)), BF16),
        pltpu.VMEM((tall, rows), F32),
        pltpu.VMEM((peers, tall, rows), F32),
        pltpu.VMEM((depth, rows), F32),
        pltpu.VMEM((-(-(n_s + 1) // 8) * 8, rows), F32),
        pltpu.VMEM((8, rows), F32),
        pltpu.VMEM((depth, rows), F32),
        pltpu.VMEM((2, width, depth), F32),
        pltpu.VMEM((others, 2, width, depth), BF16),
        pltpu.VMEM((others, 2, width, depth), BF16),
        pltpu.VMEM((n_p, count, window // n_p, wide), F32),
        pltpu.VMEM((peers, count, window // n_p, wide), F32),
        dma((others, 2)),
        dma((others, 2)),
        dma((peers,)),
        dma((peers,)),
        dma((others,)),
        dma((others,)),
        dma((peers,)),
        dma((peers,)),
    ]
    return pl.pallas_call(
        functools.partial(kernel, n_p, n_s),
        out_shape=(
            shape(queries.shape, BF16),
            shape((count, window // n_p, wide), BF16),
            shape(prompt_keys.shape, BF16),
            shape(prompt_values.shape, BF16),
            shape(resp_keys.shape, BF16),
            shape(resp_values.shape, BF16),
        ),
        in_specs=[smem] * 2 + [vmem] * 6,
        out_specs=[vmem] * 6,
        scratch_shapes=scratch,
        compiler_params=pltpu.CompilerParams(
            collective_id=0, has_side_effects=True, vmem_limit_bytes=52 * 1024 * 1024
        ),
    )(offsets, lengths, queries, prompt_keys, prompt_values, resp_keys, resp_values, cotangent)


def solution(mesh):
    return jax.shard_map(
        functools.partial(local, mesh.shape["prompt"], mesh.shape["sample"]),
        mesh=mesh,
        in_specs=(
            P("sample", None, "head"),
            P(("prompt", "sample"), "head"),
            P(("prompt", "sample"), "head"),
            P("sample", "prompt", "head"),
            P("sample", "prompt", "head"),
            P("sample", None, "head"),
            P(),
            P(),
        ),
        out_specs=(
            P("sample", None, "head"),
            P("sample", "prompt", "head"),
            P(("prompt", "sample"), "head"),
            P(("prompt", "sample"), "head"),
            P("sample", "prompt", "head"),
            P("sample", "prompt", "head"),
        ),
        check_vma=False,
    )
```

time: 216 us -> 49.6 us (0.23)
  matrix products: 73.6 us -> 0 us
  waiting for transfers between devices: 71.2 us -> 0 us
  Pallas kernels: 0 us -> 38.9 us
  blocking collectives: 27 us -> 0 us
  between operations: 14.2 us -> 0.66 us
  other arithmetic: 13.4 us -> 0 us
  local copies, waits for them, and re-layouts: 14.5 us -> 9.7 us
    dot_general x56 -> x0, matrix products: 73.6 us -> none  [the longest x8 10.9 us: visit(): jnp.einsum('qd,kd->qk', rows, key_part, preferred_element_type=jnp.float32)]
    reduce_scatter x3 -> x0, waiting for transfers between devices: 66.5 us -> none  [the longest x1 30.4 us: local(): lax.psum_scatter(key_grad, 'sample', scatter_dimension=0, tiled=True)]
    pallas_call x0 -> x1, Pallas kernels: none -> 38.9 us  [local(): pl.pallas_call(functools.partial(kernel, n_p, n_s), out_shape=(shape(quer...]
    all_gather x4 -> x0, blocking collectives: 27 us -> none  [the longest x1 12.2 us: local(): lax.all_gather(prompt_keys, 'sample', axis=0, tiled=True)]
    unnamed x26 -> x20, local copies, waits for them, and re-layouts: 0.68 us -> 9.7 us
    reshape x16 -> x0, local copies, waits for them, and re-layouts: 5.85 us -> none  [the longest x1 1.21 us: local(): sample_terms = query_grad.reshape(own_count, window, wide) + own_query_grad]
    convert_element_type x5 -> x0, other arithmetic: 5.67 us -> none  [the longest x1 1.62 us: local(): lax.psum_scatter(sample_terms, 'prompt', scatter_dimension=1, tiled=True)]
    all_gather x1 -> x0, waiting for transfers between devices: 3.44 us -> none  [joined_2(): everything = jax.tree.map(lambda part: lax.all_gather(part, axis), shard)]
  transfers between devices with their start and end apart: 4 -> 0, of which waited for: 4 -> 0; matrix products, arithmetic and copies ran while one was open for 3% -> 0% of each run, Pallas kernels for 0% -> 0%
where the time goes in v1:
time: 49.6 us; the launch traced here: 49.3 us
  Pallas kernels  38.9 us (78%)
  local copies, waits for them, and re-layouts  9.7 us (20%)
  between operations  0.66 us (1%)
    pallas_call x1, Pallas kernels, local(): pl.pallas_call(functools.partial(kernel, n_p, n_s), out_shape=(shape(quer...  38.9 us
    unnamed x20, local copies, waits for them, and re-layouts  9.7 us

profile of v1, /device:TPU:0, one launch (start us, length us, event | category | flops | bytes accessed | tf_op | source)
XLA Modules:
  0.0 49.3 jit_solution(10874112262916112637)
XLA Ops:
  0.6 0.0 copy-start
  0.6 0.9 %copy-done = bf16[2,64,1024]{2,1,0:T(8,128)(2,1)S(1)} copy-done((bf16[2,64,1024]{2,1,0:T(8,128)(2,1)S(1)}, bf16[2,64,1024]{2,1,0:T(8,128)(2,1)}, u32[]{:S(2)}) %copy-start) | copy-done | bytes 262168
  1.6 0.0 copy-start.1
  1.6 0.9 %copy-done.1 = bf16[2,64,1024]{2,1,0:T(8,128)(2,1)S(1)} copy-done((bf16[2,64,1024]{2,1,0:T(8,128)(2,1)S(1)}, bf16[2,64,1024]{2,1,0:T(8,128)(2,1)}, u32[]{:S(2)}) %copy-start.1) | copy-done | bytes 262168
  2.5 0.0 copy-start.2
  2.5 0.9 %copy-done.2 = bf16[512,128]{1,0:T(8,128)(2,1)S(1)} copy-done((bf16[512,128]{1,0:T(8,128)(2,1)S(1)}, bf16[512,128]{1,0:T(8,128)(2,1)}, u32[]{:S(2)}) %copy-start.2) | copy-done | bytes 131096
  3.4 0.0 copy-start.3
  3.4 0.9 %copy-done.3 = bf16[512,128]{1,0:T(8,128)(2,1)S(1)} copy-done((bf16[512,128]{1,0:T(8,128)(2,1)S(1)}, bf16[512,128]{1,0:T(8,128)(2,1)}, u32[]{:S(2)}) %copy-start.3) | copy-done | bytes 131096
  4.3 0.0 copy-start.4
  4.3 0.7 %copy-done.4 = s32[8]{0:T(128)S(1)} copy-done((s32[8]{0:T(128)S(1)}, s32[8]{0:T(128)}, u32[]{:S(2)}) %copy-start.4) | copy-done | bytes 56
  5.0 0.0 copy-start.5
  5.0 0.7 %copy-done.5 = s32[8]{0:T(128)S(1)} copy-done((s32[8]{0:T(128)S(1)}, s32[8]{0:T(128)}, u32[]{:S(2)}) %copy-start.5) | copy-done | bytes 56
  5.7 38.9 %shard_map.127 = (bf16[2,64,1024]{2,1,0:T(8,128)(2,1)S(1)}, bf16[2,32,1024]{2,1,0:T(8,128)(2,1)S(1)}, bf16[512,128]{1,0:T(8,128)(2,1)S(1)}, bf16[512,128]{1,0:T(...) custom-call(s32[8]{0:T(128)S(1)} %copy-done.4, s32[8]{0:T(128)S(1)} %copy-done.5, ...), custom_call_target="tpu_custom_call" | custom-call | tf_op jit(solution)/shard_map/pallas_call | solution.py:353
  44.6 0.7 %copy.20 = bf16[2,64,1024]{2,1,0:T(8,128)(2,1)} copy(bf16[2,64,1024]{2,1,0:T(8,128)(2,1)S(1)} %get-tuple-element.12) | data formatting | bytes 524288
  45.3 0.7 %copy.21 = bf16[2,32,1024]{2,1,0:T(8,128)(2,1)} copy(bf16[2,32,1024]{2,1,0:T(8,128)(2,1)S(1)} %get-tuple-element.13) | data formatting | bytes 262144
  45.9 0.7 %copy.22 = bf16[512,128]{1,0:T(8,128)(2,1)} copy(bf16[512,128]{1,0:T(8,128)(2,1)S(1)} %get-tuple-element.14) | data formatting | bytes 262144
  46.6 0.7 %copy.23 = bf16[512,128]{1,0:T(8,128)(2,1)} copy(bf16[512,128]{1,0:T(8,128)(2,1)S(1)} %get-tuple-element.15) | data formatting | bytes 262144
  47.3 0.0 copy-start.6
  47.3 0.8 %copy.24 = bf16[2,1024,128]{2,1,0:T(8,128)(2,1)} copy(bf16[2,1024,128]{2,1,0:T(8,128)(2,1)S(1)} %get-tuple-element.16) | data formatting | bytes 1048576
  48.1 0.4 copy-done.6
  48.5 0.8 %copy.25 = bf16[2,1024,128]{2,1,0:T(8,128)(2,1)} copy(bf16[2,1024,128]{2,1,0:T(8,128)(2,1)S(1)} %copy-done.6) | data formatting | bytes 1048576
Async XLA Ops:
  0.6 1.0 %copy-start = (bf16[2,64,1024]{2,1,0:T(8,128)(2,1)S(1)}, bf16[2,64,1024]{2,1,0:T(8,128)(2,1)}, u32[]{:S(2)}) copy-start(bf16[2,64,1024]{2,1,0:T(8,128)(2,1)} %q_ref.1) | copy-start | bytes 786436
  1.6 0.9 %copy-start.1 = (bf16[2,64,1024]{2,1,0:T(8,128)(2,1)S(1)}, bf16[2,64,1024]{2,1,0:T(8,128)(2,1)}, u32[]{:S(2)}) copy-start(bf16[2,64,1024]{2,1,0:T(8,128)(2,1)} %g_ref.1) | copy-start | bytes 786436
  2.5 0.9 %copy-start.2 = (bf16[512,128]{1,0:T(8,128)(2,1)S(1)}, bf16[512,128]{1,0:T(8,128)(2,1)}, u32[]{:S(2)}) copy-start(bf16[512,128]{1,0:T(8,128)(2,1)} %pk_ref.1) | copy-start | bytes 393220
  3.4 0.9 %copy-start.3 = (bf16[512,128]{1,0:T(8,128)(2,1)S(1)}, bf16[512,128]{1,0:T(8,128)(2,1)}, u32[]{:S(2)}) copy-start(bf16[512,128]{1,0:T(8,128)(2,1)} %pv_ref.1) | copy-start | bytes 393220
  4.3 0.7 %copy-start.4 = (s32[8]{0:T(128)S(1)}, s32[8]{0:T(128)}, u32[]{:S(2)}) copy-start(s32[8]{0:T(128)} %offsets.1) | copy-start | bytes 100
  5.0 0.7 %copy-start.5 = (s32[8]{0:T(128)S(1)}, s32[8]{0:T(128)}, u32[]{:S(2)}) copy-start(s32[8]{0:T(128)} %lengths.1) | copy-start | bytes 100
  47.3 1.2 %copy-start.6 = (bf16[2,1024,128]{2,1,0:T(8,128)(2,1)S(1)}, bf16[2,1024,128]{2,1,0:T(8,128)(2,1)}, u32[]{:S(2)}) copy-start(bf16[2,1024,128]{2,1,0:T(8,128)(2,1)} %get-tuple-element.17) | copy-start | bytes 1572868

commit v2 on v1

--- a/solution.py
+++ b/solution.py
@@ -25,6 +25,20 @@
 def kernel(
     n_p,
     n_s,
+    offsets_hbm,
+    lengths_hbm,
+    q_hbm,
+    pk_hbm,
+    pv_hbm,
+    rk_hbm,
+    rv_hbm,
+    g_hbm,
+    att_ref,
+    gq_ref,
+    gpk_ref,
+    gpv_ref,
+    grk_ref,
+    grv_ref,
     offsets,
     lengths,
     q_ref,
@@ -33,12 +47,6 @@
     rk_ref,
     rv_ref,
     g_ref,
-    att_ref,
-    gq_ref,
-    gpk_ref,
-    gpv_ref,
-    grk_ref,
-    grv_ref,
     kv,
     qrows,
     grows,
@@ -67,6 +75,7 @@
     kvg_recv,
     gq_send,
     gq_recv,
+    load_sem,
 ):
     count, window, wide = q_ref.shape
     width, depth = pk_ref.shape
@@ -92,6 +101,20 @@
             return to_sample(k)
         return (me_s + n_s - k) % n_s
 
+    loads = {}
+    for name, src, dst in (
+        ("offsets", offsets_hbm, offsets),
+        ("lengths", lengths_hbm, lengths),
+        ("q", q_hbm, q_ref),
+        ("rk", rk_hbm, rk_ref),
+        ("rv", rv_hbm, rv_ref),
+        ("pk", pk_hbm, pk_ref),
+        ("pv", pv_hbm, pv_ref),
+        ("g", g_hbm, g_ref),
+    ):
+        loads[name] = pltpu.make_async_copy(src, dst, load_sem.at[len(loads)])
+        loads[name].start()
+
     barrier = pltpu.get_barrier_semaphore()
     for k in range(1, n_s):
         pl.semaphore_signal(barrier, inc=1, device_id={"sample": to_sample(k)}, device_id_type=MESH)
@@ -102,31 +125,28 @@
     pl.semaphore_wait(barrier, n_s - 1 + n_p - 1)
 
     kv_copies = {}
-    for k in range(1, n_s):
-        for j, ref in enumerate((pk_ref, pv_ref)):
-            copy = pltpu.make_async_remote_copy(
-                src_ref=ref,
-                dst_ref=kv.at[k - 1, j],
-                send_sem=kv_send.at[k - 1, j],
-                recv_sem=kv_recv.at[k - 1, j],
-                device_id={"sample": to_sample(k)},
-                device_id_type=MESH,
-            )
-            copy.start()
-            kv_copies[k, j] = copy
-
-    own = [(offsets[me_s * count + r], lengths[me_s * count + r]) for r in range(count)]
-    line = lax.broadcasted_iota(jnp.int32, (window, 1), 0)
-    for r in range(count):
-        live = own[r][0] + line < own[r][1]
-        for h in range(group):
-            at = pl.ds(r * height + h * window, window)
-            head = pl.ds(h * depth, depth)
-            qrows[at, :] = q_ref[r, :, head]
-            grows[at, :] = jnp.where(live, g_ref[r, :, head].astype(F32), 0.0).astype(BF16)
-    for i in range(rows // tile):
-        at = pl.ds(i * tile, tile)
-        g_t[:, at] = grows[at, :].T
+
+    def send_kv(k, j, src, to):
+        copy = pltpu.make_async_remote_copy(
+            src_ref=src,
+            dst_ref=kv.at[k - 1, j],
+            send_sem=kv_send.at[k - 1, j],
+            recv_sem=kv_recv.at[k - 1, j],
+            device_id={"sample": to_sample(to)},
+            device_id_type=MESH,
+        )
+        copy.start()
+        kv_copies[k, j] = copy
+
+    relay = n_s == 4
+    mine = (pk_hbm, pv_hbm)
+    if relay:
+        for k, j in ((1, 0), (2, 1), (1, 1), (2, 0)):
+            send_kv(k, j, mine[j], k)
+    else:
+        for k in range(1, n_s):
+            for j in range(2):
+                send_kv(k, j, mine[j], k)
 
     def forward(seg, keys, values, p_ref, low, high, mask, first):
         size = keys.shape[0]
@@ -158,40 +178,78 @@
                 acc[depth + 1 : depth + 2, at] = acc[depth + 1 : depth + 2, at] * old + total * new
             return 0
 
-        lax.fori_loop(low, high, visit, 0)
-
+        lax.fori_loop(low, high, visit, 0, unroll=True)
+
+    def own_forward():
+        for r in range(count):
+            key_place = me_p * span + lax.broadcasted_iota(jnp.int32, (span, 1), 0)
+            row_place = own[r][0] + lax.broadcasted_iota(jnp.int32, (1, tile), 1) % window
+
+            def mask(scores):
+                return jnp.where(key_place <= row_place, scores, NEG)
+
+            forward(n_s, rk_ref.at[r], rv_ref.at[r], p_own, r * per, (r + 1) * per, mask, True)
+
+    for name in ("offsets", "lengths", "q"):
+        loads[name].wait()
+    own = [(offsets[me_s * count + r], lengths[me_s * count + r]) for r in range(count)]
+    line = lax.broadcasted_iota(jnp.int32, (window, 1), 0)
     for r in range(count):
-        key_place = me_p * span + lax.broadcasted_iota(jnp.int32, (span, 1), 0)
-        row_place = own[r][0] + lax.broadcasted_iota(jnp.int32, (1, tile), 1) % window
-
-        def mask(scores):
-            return jnp.where(key_place <= row_place, scores, NEG)
-
-        forward(n_s, rk_ref.at[r], rv_ref.at[r], p_own, r * per, (r + 1) * per, mask, True)
+        for h in range(group):
+            at = pl.ds(r * height + h * window, window)
+            head = pl.ds(h * depth, depth)
+            qrows[at, :] = q_ref[r, :, head]
+    loads["rk"].wait()
+    loads["rv"].wait()
+    own_forward()
+    if relay:
+        kv_copies[1, 0].wait_recv()
+        send_kv(3, 0, kv.at[0, 0], 2)
+        kv_copies[2, 1].wait_recv()
+        send_kv(3, 1, kv.at[1, 1], 1)
+    loads["g"].wait()
+    for r in range(count):
+        live = own[r][0] + line < own[r][1]
+        for h in range(group):
+            at = pl.ds(r * height + h * window, window)
+            head = pl.ds(h * depth, depth)
+            grows[at, :] = jnp.where(live, g_ref[r, :, head].astype(F32), 0.0).astype(BF16)
+    for i in range(rows // tile):
+        at = pl.ds(i * tile, tile)
+        g_t[:, at] = grows[at, :].T
+
+    loads["pk"].wait()
+    loads["pv"].wait()
     forward(0, pk_ref, pv_ref, p_all.at[0], 0, count * per, None, False)
+    acc_copies = []
     for k in range(1, n_s):
-        kv_copies[k, 0].wait_recv()
-        kv_copies[k, 1].wait_recv()
-        forward(
-            k, kv.at[k - 1, 0], kv.at[k - 1, 1], p_all.at[k], 0, count * per, None, False
-        )
-
-    acc_copies = []
-    for k in range(1, n_p):
-        copy = pltpu.make_async_remote_copy(
-            src_ref=acc,
-            dst_ref=acc_in.at[k - 1],
-            send_sem=acc_send.at[k - 1],
-            recv_sem=acc_recv.at[k - 1],
-            device_id={"prompt": (me_p + k) % n_p},
-            device_id_type=MESH,
-        )
-        copy.start()
-        acc_copies.append(copy)
-    for copy in acc_copies:
-        copy.wait_recv()
+        for j in range(2):
+            if not relay or (k, j) not in ((1, 0), (2, 1)):
+                kv_copies[k, j].wait_recv()
+        halves = count if k == n_s - 1 else 1
+        for half in range(halves):
+            low, high = half * count * per // halves, (half + 1) * count * per // halves
+            forward(k, kv.at[k - 1, 0], kv.at[k - 1, 1], p_all.at[k], low, high, None, False)
+            if k < n_s - 1:
+                continue
+            at = pl.ds(low * tile, (high - low) * tile)
+            for to in range(1, n_p):
+                copy = pltpu.make_async_remote_copy(
+                    src_ref=acc.at[:, at],
+                    dst_ref=acc_in.at[to - 1, :, at],
+                    send_sem=acc_send.at[to - 1, half],
+                    recv_sem=acc_recv.at[to - 1, half],
+                    device_id={"prompt": (me_p + to) % n_p},
+                    device_id_type=MESH,
+                )
+                copy.start()
+                acc_copies.append((half, copy))
 
     for i in range(rows // tile):
+        if i % per == 0:
+            for half, copy in acc_copies:
+                if half == i // per:
+                    copy.wait_recv()
         at = pl.ds(i * tile, tile)
         top = acc[depth : depth + 1, at]
         for k in range(n_p - 1):
@@ -228,12 +286,12 @@
             delta = jnp.sum(grads.astype(F32) * out_t[:, at], axis=0, keepdims=True)
             g_scaled[at, :] = grads.T
             weight_grad = dot(values[...], grads)
-            score_grad = (p_ref[:, at].astype(F32) * (weight_grad - delta)).astype(BF16)
+            score_grad = p_ref[:, at] * (weight_grad - delta).astype(BF16)
             ds[:size, at] = score_grad
             gq_t[:, at] += dot(small_t[:, :size], score_grad)
             return 0
 
-        lax.fori_loop(low, high, visit, 0)
+        lax.fori_loop(low, high, visit, 0, unroll=True)
         span_rows = slice(low * tile, high * tile)
         value_grad = dot(p_ref[:, span_rows], g_scaled[span_rows, :])
         key_grad = dot(ds[:size, span_rows], qrows[span_rows, :]) * scale
@@ -304,8 +362,20 @@
 
     for copy in kv_copies.values():
         copy.wait_send()
-    for copy in acc_copies + kvg_copies + gq_copies:
+    for copy in [copy for _, copy in acc_copies] + kvg_copies + gq_copies:
         copy.wait_send()
+
+
+def write_out(*refs):
+    sem = refs[-1]
+    half = len(refs) // 2
+    copies = [
+        pltpu.make_async_copy(refs[i], refs[half + i], sem.at[i]) for i in range(half)
+    ]
+    for copy in copies:
+        copy.start()
+    for copy in copies:
+        copy.wait()
 
 
 def local(n_p, n_s, queries, prompt_keys, prompt_values, resp_keys, resp_values, cotangent, lengths, offsets):
@@ -315,12 +385,20 @@
     rows = count * window * (wide // depth)
     tall = depth + 8
     vmem = pl.BlockSpec(memory_space=pltpu.VMEM)
-    smem = pl.BlockSpec(memory_space=pltpu.SMEM)
+    hbm = pl.BlockSpec(memory_space=pltpu.HBM)
     shape = jax.ShapeDtypeStruct
     dma = pltpu.SemaphoreType.DMA
     peers = max(n_p - 1, 1)
     others = max(n_s - 1, 1)
     scratch = [
+        pltpu.SMEM(offsets.shape, offsets.dtype),
+        pltpu.SMEM(lengths.shape, lengths.dtype),
+        pltpu.VMEM(queries.shape, BF16),
+        pltpu.VMEM(prompt_keys.shape, BF16),
+        pltpu.VMEM(prompt_values.shape, BF16),
+        pltpu.VMEM(resp_keys.shape, BF16),
+        pltpu.VMEM(resp_values.shape, BF16),
+        pltpu.VMEM(cotangent.shape, BF16),
         pltpu.VMEM((others, 2, width, depth), BF16),
         pltpu.VMEM((rows, depth), BF16),
         pltpu.VMEM((rows, depth), BF16),
@@ -343,14 +421,15 @@
         pltpu.VMEM((peers, count, window // n_p, wide), F32),
         dma((others, 2)),
         dma((others, 2)),
-        dma((peers,)),
-        dma((peers,)),
+        dma((peers, count)),
+        dma((peers, count)),
         dma((others,)),
         dma((others,)),
         dma((peers,)),
         dma((peers,)),
+        dma((8,)),
     ]
-    return pl.pallas_call(
+    results = pl.pallas_call(
         functools.partial(kernel, n_p, n_s),
         out_shape=(
             shape(queries.shape, BF16),
@@ -360,13 +439,21 @@
             shape(resp_keys.shape, BF16),
             shape(resp_values.shape, BF16),
         ),
-        in_specs=[smem] * 2 + [vmem] * 6,
+        in_specs=[hbm] * 8,
         out_specs=[vmem] * 6,
         scratch_shapes=scratch,
         compiler_params=pltpu.CompilerParams(
-            collective_id=0, has_side_effects=True, vmem_limit_bytes=52 * 1024 * 1024
+            collective_id=0, has_side_effects=True, vmem_limit_bytes=62 * 1024 * 1024
         ),
     )(offsets, lengths, queries, prompt_keys, prompt_values, resp_keys, resp_values, cotangent)
+    return pl.pallas_call(
+        write_out,
+        out_shape=tuple(shape(result.shape, result.dtype) for result in results),
+        in_specs=[vmem] * len(results),
+        out_specs=[hbm] * len(results),
+        scratch_shapes=[dma((len(results),))],
+        compiler_params=pltpu.CompilerParams(vmem_limit_bytes=4 * 1024 * 1024),
+    )(*results)
 
 
 def solution(mesh):

time: 49.6 us -> 43.6 us (0.88)
  local copies, waits for them, and re-layouts: 9.7 us -> 5.74 us
  Pallas kernels: 38.9 us -> 36.7 us
    unnamed x20 -> x12, local copies, waits for them, and re-layouts: 9.7 us -> 5.74 us
    pallas_call x1, Pallas kernels: 38.9 us -> 35.5 us  [local(): pl.pallas_call(functools.partial(kernel, n_p, n_s), out_shape=(shape(quer...]
    pallas_call x0 -> x1, Pallas kernels: none -> 1.23 us  [local(): pl.pallas_call(write_out, out_shape=tuple((shape(result.shape, result.dty...]
where the time goes in v2:
time: 43.6 us; the launch traced here: 43.3 us
  Pallas kernels  36.7 us (84%)
  local copies, waits for them, and re-layouts  5.74 us (13%)
  between operations  0.82 us (2%)
    pallas_call x1, Pallas kernels, local(): pl.pallas_call(functools.partial(kernel, n_p, n_s), out_shape=(shape(quer...  35.5 us
    unnamed x12, local copies, waits for them, and re-layouts  5.74 us
    pallas_call x1, Pallas kernels, local(): pl.pallas_call(write_out, out_shape=tuple((shape(result.shape, result.dty...  1.23 us

profile of v2, /device:TPU:0, one launch (start us, length us, event | category | flops | bytes accessed | tf_op | source)
XLA Modules:
  0.0 43.3 jit_solution(3102444345264216601)
XLA Ops:
  0.6 35.5 %shard_map.127 = (bf16[2,64,1024]{2,1,0:T(8,128)(2,1)}, bf16[2,32,1024]{2,1,0:T(8,128)(2,1)}, bf16[512,128]{1,0:T(8,128)(2,1)}, bf16[512,128]{1,0:T(8,128)(2,1)}...) custom-call(s32[8]{0:T(128)} %offsets_hbm.1, s32[8]{0:T(128)} %lengths_hbm.1, bf16[2,64,1024]{2,1,0:T(8,128)(2,1)} %q_hbm.1, ...), custom_call_target="tpu_custom_call" | custom-call | tf_op jit(solution)/shard_map/pallas_call | solution.py:432
  36.2 0.0 copy-start
  36.2 1.0 %copy-done = bf16[2,1024,128]{2,1,0:T(8,128)(2,1)S(1)} copy-done((bf16[2,1024,128]{2,1,0:T(8,128)(2,1)S(1)}, bf16[2,1024,128]{2,1,0:T(8,128)(2,1)}, u32[]{:S(2)}) %copy-start) | copy-done | bytes 524312
  37.2 0.0 copy-start.1
  37.2 1.0 %copy-done.1 = bf16[2,1024,128]{2,1,0:T(8,128)(2,1)S(1)} copy-done((bf16[2,1024,128]{2,1,0:T(8,128)(2,1)S(1)}, bf16[2,1024,128]{2,1,0:T(8,128)(2,1)}, u32[]{:S(2)}) %copy-start.1) | copy-done | bytes 524312
  38.2 0.0 copy-start.2
  38.2 0.9 %copy-done.2 = bf16[2,64,1024]{2,1,0:T(8,128)(2,1)S(1)} copy-done((bf16[2,64,1024]{2,1,0:T(8,128)(2,1)S(1)}, bf16[2,64,1024]{2,1,0:T(8,128)(2,1)}, u32[]{:S(2)}) %copy-start.2) | copy-done | bytes 262168
  39.2 0.0 copy-start.3
  39.2 0.9 %copy-done.3 = bf16[2,32,1024]{2,1,0:T(8,128)(2,1)S(1)} copy-done((bf16[2,32,1024]{2,1,0:T(8,128)(2,1)S(1)}, bf16[2,32,1024]{2,1,0:T(8,128)(2,1)}, u32[]{:S(2)}) %copy-start.3) | copy-done | bytes 131096
  40.1 0.0 copy-start.4
  40.1 0.9 %copy-done.4 = bf16[512,128]{1,0:T(8,128)(2,1)S(1)} copy-done((bf16[512,128]{1,0:T(8,128)(2,1)S(1)}, bf16[512,128]{1,0:T(8,128)(2,1)}, u32[]{:S(2)}) %copy-start.4) | copy-done | bytes 131096
  41.0 0.0 copy-start.5
  41.0 0.9 %copy-done.5 = bf16[512,128]{1,0:T(8,128)(2,1)S(1)} copy-done((bf16[512,128]{1,0:T(8,128)(2,1)S(1)}, bf16[512,128]{1,0:T(8,128)(2,1)}, u32[]{:S(2)}) %copy-start.5) | copy-done | bytes 131096
  41.9 1.2 %shard_map.128 = (bf16[2,64,1024]{2,1,0:T(8,128)(2,1)}, bf16[2,32,1024]{2,1,0:T(8,128)(2,1)}, bf16[512,128]{1,0:T(8,128)(2,1)}, bf16[512,128]{1,0:T(8,128)(2,1)}...) custom-call(bf16[2,64,1024]{2,1,0:T(8,128)(2,1)S(1)} %copy-done.2, bf16[2,32,1024]{2,1,0:T(8,128)(2,1)S(1)} %copy-done.3, ...), custom_call_target="tpu_custom_call" | custom-call | tf_op jit(solution)/shard_map/pallas_call | solution.py:449
Async XLA Ops:
  36.2 1.0 %copy-start = (bf16[2,1024,128]{2,1,0:T(8,128)(2,1)S(1)}, bf16[2,1024,128]{2,1,0:T(8,128)(2,1)}, u32[]{:S(2)}) copy-start(bf16[2,1024,128]{2,1,0:T(8,128)(2,1)} %get-tuple-element.16.refs_4_) | copy-start | bytes 1572868
  37.2 1.0 %copy-start.1 = (bf16[2,1024,128]{2,1,0:T(8,128)(2,1)S(1)}, bf16[2,1024,128]{2,1,0:T(8,128)(2,1)}, u32[]{:S(2)}) copy-start(bf16[2,1024,128]{2,1,0:T(8,128)(2,1)} %get-tuple-element.17.refs_5_) | copy-start | bytes 1572868
  38.2 0.9 %copy-start.2 = (bf16[2,64,1024]{2,1,0:T(8,128)(2,1)S(1)}, bf16[2,64,1024]{2,1,0:T(8,128)(2,1)}, u32[]{:S(2)}) copy-start(bf16[2,64,1024]{2,1,0:T(8,128)(2,1)} %get-tuple-element.12.refs_0_) | copy-start | bytes 786436
  39.2 0.9 %copy-start.3 = (bf16[2,32,1024]{2,1,0:T(8,128)(2,1)S(1)}, bf16[2,32,1024]{2,1,0:T(8,128)(2,1)}, u32[]{:S(2)}) copy-start(bf16[2,32,1024]{2,1,0:T(8,128)(2,1)} %get-tuple-element.13.refs_1_) | copy-start | bytes 393220
  40.1 0.9 %copy-start.4 = (bf16[512,128]{1,0:T(8,128)(2,1)S(1)}, bf16[512,128]{1,0:T(8,128)(2,1)}, u32[]{:S(2)}) copy-start(bf16[512,128]{1,0:T(8,128)(2,1)} %get-tuple-element.14.refs_2_) | copy-start | bytes 393220
  41.0 0.9 %copy-start.5 = (bf16[512,128]{1,0:T(8,128)(2,1)S(1)}, bf16[512,128]{1,0:T(8,128)(2,1)}, u32[]{:S(2)}) copy-start(bf16[512,128]{1,0:T(8,128)(2,1)} %get-tuple-element.15.refs_3_) | copy-start | bytes 393220

commit v3 on v2

--- a/solution.py
+++ b/solution.py
@@ -33,6 +33,12 @@
     rk_hbm,
     rv_hbm,
     g_hbm,
+    att_hbm,
+    gq_hbm,
+    gpk_hbm,
+    gpv_hbm,
+    grk_hbm,
+    grv_hbm,
     att_ref,
     gq_ref,
     gpk_ref,
@@ -76,6 +82,7 @@
     gq_send,
     gq_recv,
     load_sem,
+    store_sem,
 ):
     count, window, wide = q_ref.shape
     width, depth = pk_ref.shape
@@ -123,6 +130,12 @@
             barrier, inc=1, device_id={"prompt": (me_p + k) % n_p}, device_id_type=MESH
         )
     pl.semaphore_wait(barrier, n_s - 1 + n_p - 1)
+
+    stores = []
+
+    def store(src, dst):
+        stores.append(pltpu.make_async_copy(src, dst, store_sem.at[len(stores)]))
+        stores[-1].start()
 
     kv_copies = {}
 
@@ -275,6 +288,8 @@
             block = by_row[part_h * window : (part_h + 1) * window]
             att_ref[r, :, pl.ds(h * depth, depth)] = jnp.where(live, block, 0.0).astype(BF16)
 
+    store(att_ref, att_hbm)
+
     def backward(seg, keys, values, p_ref, low, high):
         size = keys.shape[0]
         small_t[:, :size] = keys[...].T
@@ -323,6 +338,8 @@
         )
         grk_ref[r] = key_grad.astype(BF16)
         grv_ref[r] = value_grad.astype(BF16)
+        store(grk_ref.at[r], grk_hbm.at[r])
+        store(grv_ref.at[r], grv_hbm.at[r])
 
     for i in range(rows // tile):
         at = pl.ds(i * tile, tile)
@@ -348,17 +365,21 @@
         gq_copies.append(copy)
     for copy in kvg_copies:
         copy.wait_recv()
-    for j, ref in enumerate((gpk_ref, gpv_ref)):
+    for j, (ref, out) in enumerate(((gpk_ref, gpk_hbm), (gpv_ref, gpv_hbm))):
         total = kvg_own[j]
         for k in range(n_s - 1):
             total = total + kvg_in[k, j].astype(F32)
         ref[...] = total.astype(BF16)
+        store(ref, out)
     for copy in gq_copies:
         copy.wait_recv()
     total = gq_out[me_p]
     for k in range(n_p - 1):
         total = total + gq_in[k]
     gq_ref[...] = total.astype(BF16)
+    store(gq_ref, gq_hbm)
+    for copy in stores:
+        copy.wait()
 
     for copy in kv_copies.values():
         copy.wait_send()
@@ -384,13 +405,18 @@
     span = resp_keys.shape[1]
     rows = count * window * (wide // depth)
     tall = depth + 8
-    vmem = pl.BlockSpec(memory_space=pltpu.VMEM)
     hbm = pl.BlockSpec(memory_space=pltpu.HBM)
     shape = jax.ShapeDtypeStruct
     dma = pltpu.SemaphoreType.DMA
     peers = max(n_p - 1, 1)
     others = max(n_s - 1, 1)
     scratch = [
+        pltpu.VMEM(queries.shape, BF16),
+        pltpu.VMEM((count, window // n_p, wide), BF16),
+        pltpu.VMEM(prompt_keys.shape, BF16),
+        pltpu.VMEM(prompt_values.shape, BF16),
+        pltpu.VMEM(resp_keys.shape, BF16),
+        pltpu.VMEM(resp_values.shape, BF16),
         pltpu.SMEM(offsets.shape, offsets.dtype),
         pltpu.SMEM(lengths.shape, lengths.dtype),
         pltpu.VMEM(queries.shape, BF16),
@@ -428,6 +454,7 @@
         dma((peers,)),
         dma((peers,)),
         dma((8,)),
+        dma((4 + 2 * count,)),
     ]
     results = pl.pallas_call(
         functools.partial(kernel, n_p, n_s),
@@ -440,7 +467,7 @@
             shape(resp_values.shape, BF16),
         ),
         in_specs=[hbm] * 8,
-        out_specs=[vmem] * 6,
+        out_specs=[hbm] * 6,
         scratch_shapes=scratch,
         compiler_params=pltpu.CompilerParams(
             collective_id=0, has_side_effects=True, vmem_limit_bytes=62 * 1024 * 1024
@@ -449,10 +476,10 @@
     return pl.pallas_call(
         write_out,
         out_shape=tuple(shape(result.shape, result.dtype) for result in results),
-        in_specs=[vmem] * len(results),
+        in_specs=[hbm] * len(results),
         out_specs=[hbm] * len(results),
         scratch_shapes=[dma((len(results),))],
-        compiler_params=pltpu.CompilerParams(vmem_limit_bytes=4 * 1024 * 1024),
+        compiler_params=pltpu.CompilerParams(vmem_limit_bytes=62 * 1024 * 1024),
     )(*results)
 
 

time: 43.6 us -> 88.8 us (2.04)
  Pallas kernels: 36.7 us -> 87.8 us
  local copies, waits for them, and re-layouts: 5.74 us -> 0 us
    pallas_call x1, Pallas kernels: 1.23 us -> 52.8 us  [local(): pl.pallas_call(write_out, out_shape=tuple((shape(result.shape, result.dty...]
    unnamed x12 -> x0, local copies, waits for them, and re-layouts: 5.74 us -> none
where the time goes in v3:
time: 88.8 us; the launch traced here: 88.6 us
  Pallas kernels  87.8 us (99%)
    pallas_call x1, Pallas kernels, local(): pl.pallas_call(write_out, out_shape=tuple((shape(result.shape, result.dty...  52.8 us
    pallas_call x1, Pallas kernels, local(): pl.pallas_call(functools.partial(kernel, n_p, n_s), out_shape=(shape(quer...  35.1 us

profile of v3, /device:TPU:0, one launch (start us, length us, event | category | flops | bytes accessed | tf_op | source)
XLA Modules:
  0.0 88.6 jit_solution(9021541272796462008)
XLA Ops:
  0.6 35.1 %shard_map.127 = (bf16[2,64,1024]{2,1,0:T(8,128)(2,1)}, bf16[2,32,1024]{2,1,0:T(8,128)(2,1)}, bf16[512,128]{1,0:T(8,128)(2,1)}, bf16[512,128]{1,0:T(8,128)(2,1)}...) custom-call(s32[8]{0:T(128)} %offsets_hbm.1, s32[8]{0:T(128)} %lengths_hbm.1, bf16[2,64,1024]{2,1,0:T(8,128)(2,1)} %q_hbm.1, ...), custom_call_target="tpu_custom_call" | custom-call | tf_op jit(solution)/shard_map/pallas_call | solution.py:459
  35.7 52.8 %shard_map.128 = (bf16[2,64,1024]{2,1,0:T(8,128)(2,1)}, bf16[2,32,1024]{2,1,0:T(8,128)(2,1)}, bf16[512,128]{1,0:T(8,128)(2,1)}, bf16[512,128]{1,0:T(8,128)(2,1)}...) custom-call(bf16[2,64,1024]{2,1,0:T(8,128)(2,1)} %get-tuple-element.12.refs_0_, ...), custom_call_target="tpu_custom_call" | custom-call | tf_op jit(solution)/shard_map/pallas_call | solution.py:476

commit v4 on v3

--- a/solution.py
+++ b/solution.py
@@ -90,7 +90,7 @@
     group = wide // depth
     height = window * group
     rows = count * height
-    tile = math.gcd(height, 256)
+    tile = math.gcd(height, 512)
     per = height // tile
     scale = 1.0 / math.sqrt(depth)
     c = scale * math.log2(math.e)
@@ -387,15 +387,17 @@
         copy.wait_send()
 
 
-def write_out(*refs):
-    sem = refs[-1]
-    half = len(refs) // 2
-    copies = [
-        pltpu.make_async_copy(refs[i], refs[half + i], sem.at[i]) for i in range(half)
-    ]
-    for copy in copies:
+def write_out(count, *refs):
+    sources, targets, held = refs[:count], refs[count : 2 * count], refs[2 * count : 3 * count]
+    load_sem, store_sem = refs[3 * count :]
+    loads = [pltpu.make_async_copy(sources[i], held[i], load_sem.at[i]) for i in range(count)]
+    stores = [pltpu.make_async_copy(held[i], targets[i], store_sem.at[i]) for i in range(count)]
+    for copy in loads:
         copy.start()
-    for copy in copies:
+    for load, store in zip(loads, stores):
+        load.wait()
+        store.start()
+    for copy in stores:
         copy.wait()
 
 
@@ -474,11 +476,12 @@
         ),
     )(offsets, lengths, queries, prompt_keys, prompt_values, resp_keys, resp_values, cotangent)
     return pl.pallas_call(
-        write_out,
+        functools.partial(write_out, len(results)),
         out_shape=tuple(shape(result.shape, result.dtype) for result in results),
         in_specs=[hbm] * len(results),
         out_specs=[hbm] * len(results),
-        scratch_shapes=[dma((len(results),))],
+        scratch_shapes=[pltpu.VMEM(result.shape, result.dtype) for result in results]
+        + [dma((len(results),))] * 2,
         compiler_params=pltpu.CompilerParams(vmem_limit_bytes=62 * 1024 * 1024),
     )(*results)
 

time: 88.8 us -> 35.9 us (0.40)
  Pallas kernels: 87.8 us -> 35.1 us
    pallas_call x1, Pallas kernels: 52.8 us -> 2.36 us  [local(): pl.pallas_call(functools.partial(write_out, len(results)), out_shape=tupl...]
    pallas_call x1, Pallas kernels: 35.1 us -> 32.7 us  [local(): pl.pallas_call(functools.partial(kernel, n_p, n_s), out_shape=(shape(quer...]
where the time goes in v4:
time: 35.9 us; the launch traced here: 35.7 us
  Pallas kernels  35.1 us (98%)
  between operations  0.64 us (2%)
    pallas_call x1, Pallas kernels, local(): pl.pallas_call(functools.partial(kernel, n_p, n_s), out_shape=(shape(quer...  32.7 us
    pallas_call x1, Pallas kernels, local(): pl.pallas_call(functools.partial(write_out, len(results)), out_shape=tupl...  2.36 us

profile of v4, /device:TPU:0, one launch (start us, length us, event | category | flops | bytes accessed | tf_op | source)
XLA Modules:
  0.0 35.7 jit_solution(16062602300409202281)
XLA Ops:
  0.6 32.7 %shard_map.127 = (bf16[2,64,1024]{2,1,0:T(8,128)(2,1)}, bf16[2,32,1024]{2,1,0:T(8,128)(2,1)}, bf16[512,128]{1,0:T(8,128)(2,1)}, bf16[512,128]{1,0:T(8,128)(2,1)}...) custom-call(s32[8]{0:T(128)} %offsets_hbm.1, s32[8]{0:T(128)} %lengths_hbm.1, bf16[2,64,1024]{2,1,0:T(8,128)(2,1)} %q_hbm.1, ...), custom_call_target="tpu_custom_call" | custom-call | tf_op jit(solution)/shard_map/pallas_call | solution.py:461
  33.4 2.4 %shard_map.128 = (bf16[2,64,1024]{2,1,0:T(8,128)(2,1)}, bf16[2,32,1024]{2,1,0:T(8,128)(2,1)}, bf16[512,128]{1,0:T(8,128)(2,1)}, bf16[512,128]{1,0:T(8,128)(2,1)}...) custom-call(bf16[2,64,1024]{2,1,0:T(8,128)(2,1)} %get-tuple-element.12.refs_0_, ...), custom_call_target="tpu_custom_call" | custom-call | tf_op jit(solution)/shard_map/pallas_call | solution.py:478
